TPU v7x, 256 devices: a whole 4x4x8 slice. The times are simulated.
256 devices in a mesh: group: 2 (over y_lo), branch: 16 (over y_hi, x, core), tensor: 8 (over z).
Axes of the slice: x: 4, y: 4 (y_hi: 2, y_lo: 2; y = y_hi * 2 + y_lo), z: 8, core: 2. Of those that a mesh axis runs over, the one named last changes fastest.
Arguments:
- queries: bfloat16 [8192, 8192], P(('group', 'branch'), 'tensor'), parts along dimension 0, may hold values from -160 to 160
- prefix_cache: bfloat16 [2, 3072, 1024], P(None, 'group', 'tensor'), parts along dimension 1, may hold values from -5 to 5
- prior_cache: bfloat16 [2, 8192, 1024], P(None, ('group', 'branch'), 'tensor'), parts along dimension 1, may hold values from -5 to 5
- fresh_cache: bfloat16 [2, 8192, 1024], P(None, ('group', 'branch'), 'tensor'), parts along dimension 1, may hold values from -5 to 5
- visible: int32 [32, 16], P('group'), parts along dimension 0, may hold values 0 or 1
- turn_order: int32 [32], P('group'), parts along dimension 0, may hold values from 0 to 15, each once
- output_weight: bfloat16 [8192, 8192], P('tensor', 'branch'), may hold values from -0.0625 to 0.0625
Outputs:
- projected: bfloat16 [8192, 8192], P(('group', 'branch'), 'tensor'), parts along dimension 0
There are 2 independent parts, one for each index of `group`. A program takes and returns all parts, laid end to end along the dimension named above; an argument that names none is the same for every part. Nothing has to cross between parts.
Inputs may be any that keep to these rules, and one draw needn't show every extreme that they name: `turn_order`: each of 0 to 15 once.
All inputs are finite; a program needn't handle non-finite values.
Results may differ from a plain program's by a relative error of at most 0.015.
Values may be sent and summed in bfloat16 or wider, within the bound.
A program may use at most 64 MiB of HBM per device.

v0:
```python
import math
import jax
import jax.numpy as jnp
from jax import lax
from jax.sharding import PartitionSpec as P

HD = 128
NEGATIVE = -1e30


def largest_divisor(total_rows, ceiling):
    chosen = 1
    for candidate in range(1, min(total_rows, ceiling) + 1):
        if total_rows % candidate == 0:
            chosen = candidate
    return chosen


def update_state(running, query_heads, key_rows, value_rows, allowed):
    peak_old, total_old, summed_old = running
    scores = jnp.einsum(
        "qhgd,khd->hgqk", query_heads, key_rows, preferred_element_type=jnp.float32
    ) / math.sqrt(HD)
    if allowed is None:
        masked = scores
    else:
        masked = jnp.where(allowed, scores, NEGATIVE)
    peak_new = jnp.maximum(peak_old, jnp.max(masked, axis=-1))
    weights = jnp.exp(masked - peak_new[..., None])
    if allowed is not None:
        weights = jnp.where(allowed, weights, 0.0)
    factor = jnp.exp(peak_old - peak_new)
    total_new = total_old * factor + jnp.sum(weights, axis=-1)
    summed_new = summed_old * factor[..., None] + jnp.einsum(
        "hgqk,khd->hgqd",
        weights.astype(jnp.bfloat16),
        value_rows,
        preferred_element_type=jnp.float32,
    )
    return (peak_new, total_new, summed_new)


def sweep(running, query_heads, key_rows, value_rows, allow_rows):
    row_count = key_rows.shape[0]
    block_rows = largest_divisor(row_count, 1024)
    if block_rows == row_count:
        return update_state(running, query_heads, key_rows, value_rows, allow_rows(0, row_count))
    block_count = row_count // block_rows
    key_blocks = key_rows.reshape(block_count, block_rows, key_rows.shape[1], key_rows.shape[2])
    value_blocks = value_rows.reshape(
        block_count, block_rows, value_rows.shape[1], value_rows.shape[2]
    )

    def advance(state, inputs):
        key_block, value_block, position = inputs
        return (
            update_state(
                state,
                query_heads,
                key_block,
                value_block,
                allow_rows(position * block_rows, block_rows),
            ),
            None,
        )

    running, unused = lax.scan(
        advance, running, (key_blocks, value_blocks, jnp.arange(block_count, dtype=jnp.int32))
    )
    return running


def per_device(queries, prefix_cache, prior_cache, fresh_cache, visible, turn_order, output_weight):
    message_rows = queries.shape[0]
    local_heads = queries.shape[1] // HD
    local_groups = prefix_cache.shape[2] // HD
    sharing = local_heads // local_groups
    query_heads = queries.reshape(message_rows, local_groups, sharing, HD)
    agent_index = lax.axis_index("branch")
    agent_count = visible.shape[0]
    seen_row = lax.dynamic_slice_in_dim(visible, agent_index, 1, 0)[0]
    own_turn = lax.dynamic_slice_in_dim(turn_order, agent_index, 1, 0)[0]
    positions = jnp.arange(message_rows, dtype=jnp.int32)
    agent_ids = jnp.arange(agent_count, dtype=jnp.int32)

    def split_cache(cache):
        return (cache[0].reshape(-1, local_groups, HD), cache[1].reshape(-1, local_groups, HD))

    def whole_rows(offset, count):
        return None

    start_state = (
        jnp.full((local_groups, sharing, message_rows), NEGATIVE, jnp.float32),
        jnp.zeros((local_groups, sharing, message_rows), jnp.float32),
        jnp.zeros((local_groups, sharing, message_rows, HD), jnp.float32),
    )
    prefix_keys, prefix_values = split_cache(prefix_cache)
    prefix_state = sweep(start_state, query_heads, prefix_keys, prefix_values, whole_rows)

    def add_messages(running, pieces, root):
        prior_keys, prior_values = split_cache(pieces[0])
        fresh_keys, fresh_values = split_cache(pieces[1])

        def locate(offset, count):
            row_index = root + offset + jnp.arange(count, dtype=jnp.int32)
            owner_ids = row_index // message_rows
            onehot = owner_ids[:, None] == agent_ids[None, :]
            return (row_index, owner_ids, onehot)

        def prior_allowed(offset, count):
            row_index, owner_ids, onehot = locate(offset, count)
            visible_rows = jnp.sum(jnp.where(onehot, seen_row[None, :], 0), axis=1) > 0
            return visible_rows[None, :]

        def fresh_allowed(offset, count):
            row_index, owner_ids, onehot = locate(offset, count)
            turn_values = jnp.sum(jnp.where(onehot, turn_order[None, :], 0), axis=1)
            earlier = turn_values < own_turn
            causal = (owner_ids == agent_index)[None, :] & (
                (row_index % message_rows)[None, :] <= positions[:, None]
            )
            return earlier[None, :] | causal

        running = sweep(running, query_heads, prior_keys, prior_values, prior_allowed)
        return sweep(running, query_heads, fresh_keys, fresh_values, fresh_allowed)

    peak_final, total_final, summed_final = add_messages(
        prefix_state,
        (
            lax.all_gather(prior_cache, "branch", axis=1, tiled=True),
            lax.all_gather(fresh_cache, "branch", axis=1, tiled=True),
        ),
        jnp.int32(0),
    )
    heads_out = (summed_final / total_final[..., None]).astype(jnp.bfloat16)
    attention = jnp.transpose(heads_out, (2, 0, 1, 3)).reshape(message_rows, local_heads * HD)
    product = jnp.dot(
        lax.all_gather(attention, "branch", axis=0, tiled=True),
        output_weight,
        preferred_element_type=jnp.float32,
    )
    partial_columns = product.astype(jnp.bfloat16).astype(jnp.float32)
    column_totals = lax.psum_scatter(
        partial_columns.astype(jnp.bfloat16), "tensor", scatter_dimension=1, tiled=True
    )
    result = lax.all_to_all(column_totals, "branch", split_axis=0, concat_axis=1, tiled=True)
    return result


def solution(mesh):
    return jax.shard_map(
        per_device,
        mesh=mesh,
        in_specs=(
            P(("group", "branch"), "tensor"),
            P(None, "group", "tensor"),
            P(None, ("group", "branch"), "tensor"),
            P(None, ("group", "branch"), "tensor"),
            P("group", None),
            P("group"),
            P("tensor", "branch"),
        ),
        out_specs=P(("group", "branch"), "tensor"),
        check_vma=False,
    )
```

profile of v0, /device:TPU:1, one launch (start us, length us, event | category | flops | bytes accessed | tf_op | source)
XLA Modules:
  0.0 348.3 jit_solution(16154351550768117709)
XLA Ops:
  10.8 18.8 %while.51 = (s32[]{:T(128)}, f32[1,8,256]{2,1,0:T(8,128)S(1)}, f32[1,8,256]{2,1,0:T(8,128)S(1)}, f32[1,8,256,128]{3,2,1,0:T(8,128)S(1)}, bf16[2,768,1,128]{3,1,2...) while((s32[]{:T(128)}, f32[1,8,256]{2,1,0:T(8,128)S(1)}, ...), condition=%wide.region_3.4_spmd.clone, body=%wide.region_0.3_spmd.clone.sunk | while | flops 818688000 | bytes 47186060 | solution.py:67
  10.8 3.6 %bitcast_reduce_fusion.5 = (f32[8,256]{1,0:T(8,128)S(1)}, f32[768,256,8]{1,0,2:T(8,128)}) fusion(bf16[256,1,8,128]{3,0,2,1:T(8,128)(2,1)S(1)} %get-tuple-element.758, bf16[2,768,1,128]{3,1,2,0:T(8,128)(2,1)S(1)} %get-tuple-element.757, s32[]{:T(128)} %get-tuple-element.744), kind=kOutput, calls=%fused_computation.88.clone.1 | convolution fusion | flops 405796864 | bytes 7020548 | tf_op jit(solution)/shard_map/while/body/eval_jaxpr/qhgd,khd->hgqk/dot_general | solution.py:21
  14.5 4.5 %fusion.130 = f32[1,8,256,128]{3,2,1,0:T(8,128)S(1)} fusion(f32[768,256,8]{1,0,2:T(8,128)} %get-tuple-element.733, f32[8,256]{1,0:T(8,128)S(1)} %bitcast.284, f32[1,8,256,128]{3,2,1,0:T(8,128)S(1)} %get-tuple-element.747, f32[8,256]{1,0:T(8,128)S(1)} %get-tuple-element.734, pred[]{:T(512)S(6)} %compare.35, ...), kind=kOutput, calls=%fused_computation.97.clone.1 | convolution fusion | flops 408158208 | bytes 8601605 | tf_op jit(solution)/shard_map/while/body/eval_jaxpr/hgqk,khd->hgqd/dot_general | solution.py:34
  20.1 3.6 %bitcast_reduce_fusion.5 = (f32[8,256]{1,0:T(8,128)S(1)}, f32[768,256,8]{1,0,2:T(8,128)}) fusion(bf16[256,1,8,128]{3,0,2,1:T(8,128)(2,1)S(1)} %get-tuple-element.758, bf16[2,768,1,128]{3,1,2,0:T(8,128)(2,1)S(1)} %get-tuple-element.757, s32[]{:T(128)} %get-tuple-element.744), kind=kOutput, calls=%fused_computation.88.clone.1 | convolution fusion | flops 405796864 | bytes 7020548 | tf_op jit(solution)/shard_map/while/body/eval_jaxpr/qhgd,khd->hgqk/dot_general | solution.py:21
  23.8 4.6 %fusion.130 = f32[1,8,256,128]{3,2,1,0:T(8,128)S(1)} fusion(f32[768,256,8]{1,0,2:T(8,128)} %get-tuple-element.733, f32[8,256]{1,0:T(8,128)S(1)} %bitcast.284, f32[1,8,256,128]{3,2,1,0:T(8,128)S(1)} %get-tuple-element.747, f32[8,256]{1,0:T(8,128)S(1)} %get-tuple-element.734, pred[]{:T(512)S(6)} %compare.35, ...), kind=kOutput, calls=%fused_computation.97.clone.1 | convolution fusion | flops 408158208 | bytes 8601605 | tf_op jit(solution)/shard_map/while/body/eval_jaxpr/hgqk,khd->hgqd/dot_general | solution.py:34
  30.9 37.0 %all-gather.4.cloned.1.call-done = bf16[2,4096,128]{2,1,0:T(8,128)(2,1)} async-done(((bf16[2,256,128]{2,1,0:T(8,128)(2,1)}), bf16[2,4096,128]{2,1,0:T(8,128)(2,1)}) %all-gather.4.cloned.1.call-update) | async-done | bytes 2097168 | tf_op jit(solution)/shard_map/all_gather | solution.py:130
  67.9 3.0 fusion.93
  70.9 42.6 %while.49 = (s32[]{:T(128)}, f32[1,8,256]{2,1,0:T(8,128)S(1)}, f32[1,8,256]{2,1,0:T(8,128)S(1)}, f32[1,8,256,128]{3,2,1,0:T(8,128)S(1)}, s32[4]{0:T(128)S(1)}, /...) while((s32[]{:T(128)}, f32[1,8,256]{2,1,0:T(8,128)S(1)}, ...), condition=%wide.region_8.9_spmd.clone, body=%wide.region_4.8_spmd.clone.sunk | while | flops 1101600768 | bytes 28465352 | solution.py:67
  74.8 4.2 %fusion.118 = f32[1,8,256,128]{3,2,1,0:T(8,128)S(1)} fusion(f32[1024,256,8]{1,0,2:T(8,128)S(1)} %get-tuple-element.705, f32[8,256]{1,0:T(8,128)S(1)} %bitcast.288, pred[1024]{0:T(1024)(128)(4,1)S(1)} %broadcast_compare_fusion.5, f32[1,8,256,128]{3,2,1,0:T(8,128)S(1)} %get-tuple-element.776, f32[8,256]{1,0:T(8,128)S(1)} %get-tuple-element.706, ...), kind=kOutput, calls=%fused_computation.15.clone.1 | convolution fusion | flops 547880960 | bytes 10766848 | tf_op jit(solution)/shard_map/while/body/eval_jaxpr/hgqk,khd->hgqd/dot_general | solution.py:34
  85.4 4.2 %fusion.118 = f32[1,8,256,128]{3,2,1,0:T(8,128)S(1)} fusion(f32[1024,256,8]{1,0,2:T(8,128)S(1)} %get-tuple-element.705, f32[8,256]{1,0:T(8,128)S(1)} %bitcast.288, pred[1024]{0:T(1024)(128)(4,1)S(1)} %broadcast_compare_fusion.5, f32[1,8,256,128]{3,2,1,0:T(8,128)S(1)} %get-tuple-element.776, f32[8,256]{1,0:T(8,128)S(1)} %get-tuple-element.706, ...), kind=kOutput, calls=%fused_computation.15.clone.1 | convolution fusion | flops 547880960 | bytes 10766848 | tf_op jit(solution)/shard_map/while/body/eval_jaxpr/hgqk,khd->hgqd/dot_general | solution.py:34
  96.0 4.2 %fusion.118 = f32[1,8,256,128]{3,2,1,0:T(8,128)S(1)} fusion(f32[1024,256,8]{1,0,2:T(8,128)S(1)} %get-tuple-element.705, f32[8,256]{1,0:T(8,128)S(1)} %bitcast.288, pred[1024]{0:T(1024)(128)(4,1)S(1)} %broadcast_compare_fusion.5, f32[1,8,256,128]{3,2,1,0:T(8,128)S(1)} %get-tuple-element.776, f32[8,256]{1,0:T(8,128)S(1)} %get-tuple-element.706, ...), kind=kOutput, calls=%fused_computation.15.clone.1 | convolution fusion | flops 547880960 | bytes 10766848 | tf_op jit(solution)/shard_map/while/body/eval_jaxpr/hgqk,khd->hgqd/dot_general | solution.py:34
  104.1 2.6 bitcast_reduce_fusion.4
  106.7 4.2 %fusion.118 = f32[1,8,256,128]{3,2,1,0:T(8,128)S(1)} fusion(f32[1024,256,8]{1,0,2:T(8,128)S(1)} %get-tuple-element.705, f32[8,256]{1,0:T(8,128)S(1)} %bitcast.288, pred[1024]{0:T(1024)(128)(4,1)S(1)} %broadcast_compare_fusion.5, f32[1,8,256,128]{3,2,1,0:T(8,128)S(1)} %get-tuple-element.776, f32[8,256]{1,0:T(8,128)S(1)} %get-tuple-element.706, ...), kind=kOutput, calls=%fused_computation.15.clone.1 | convolution fusion | flops 547880960 | bytes 10766848 | tf_op jit(solution)/shard_map/while/body/eval_jaxpr/hgqk,khd->hgqd/dot_general | solution.py:34
  113.5 9.6 %all-gather.6.cloned.1.call-done = bf16[2,4096,128]{2,1,0:T(8,128)(2,1)} async-done(((bf16[2,256,128]{2,1,0:T(8,128)(2,1)}), bf16[2,4096,128]{2,1,0:T(8,128)(2,1)}) %all-gather.6.cloned.1.call-update) | async-done | bytes 2097168 | tf_op jit(solution)/shard_map/all_gather | solution.py:131
  123.1 3.0 fusion.92
  126.1 44.2 %while.50 = (s32[]{:T(128)}, f32[1,8,256]{2,1,0:T(8,128)S(1)}, f32[1,8,256]{2,1,0:T(8,128)S(1)}, f32[1,8,256,128]{3,2,1,0:T(8,128)S(1)}, s32[4]{0:T(128)S(1)}, /...) while((s32[]{:T(128)}, f32[1,8,256]{2,1,0:T(8,128)S(1)}, ...), condition=%wide.region_13.14_spmd.clone, body=%wide.region_9.13_spmd.clone.sunk | while | flops 1102416896 | bytes 29521128 | solution.py:67
  131.4 3.7 %fusion.125 = f32[1,8,256,128]{3,2,1,0:T(8,128)S(1)} fusion(f32[1024,256,8]{1,0,2:T(8,128)S(1)} %get-tuple-element.722, f32[8,256]{1,0:T(8,128)S(1)} %bitcast.290, pred[256,1024]{0,1:T(8,128)(4,1)S(1)} %fusion.121, f32[1,8,256,128]{3,2,1,0:T(8,128)S(1)} %get-tuple-element.811, f32[8,256]{1,0:T(8,128)S(1)} %get-tuple-element.723, ...), kind=kOutput, calls=%fused_computation.52.clone.1 | convolution fusion | flops 547880960 | bytes 11026944 | tf_op jit(solution)/shard_map/while/body/eval_jaxpr/hgqk,khd->hgqd/dot_general | solution.py:34
  142.4 3.7 %fusion.125 = f32[1,8,256,128]{3,2,1,0:T(8,128)S(1)} fusion(f32[1024,256,8]{1,0,2:T(8,128)S(1)} %get-tuple-element.722, f32[8,256]{1,0:T(8,128)S(1)} %bitcast.290, pred[256,1024]{0,1:T(8,128)(4,1)S(1)} %fusion.121, f32[1,8,256,128]{3,2,1,0:T(8,128)S(1)} %get-tuple-element.811, f32[8,256]{1,0:T(8,128)S(1)} %get-tuple-element.723, ...), kind=kOutput, calls=%fused_computation.52.clone.1 | convolution fusion | flops 547880960 | bytes 11026944 | tf_op jit(solution)/shard_map/while/body/eval_jaxpr/hgqk,khd->hgqd/dot_general | solution.py:34
  153.5 3.7 %fusion.125 = f32[1,8,256,128]{3,2,1,0:T(8,128)S(1)} fusion(f32[1024,256,8]{1,0,2:T(8,128)S(1)} %get-tuple-element.722, f32[8,256]{1,0:T(8,128)S(1)} %bitcast.290, pred[256,1024]{0,1:T(8,128)(4,1)S(1)} %fusion.121, f32[1,8,256,128]{3,2,1,0:T(8,128)S(1)} %get-tuple-element.811, f32[8,256]{1,0:T(8,128)S(1)} %get-tuple-element.723, ...), kind=kOutput, calls=%fused_computation.52.clone.1 | convolution fusion | flops 547880960 | bytes 11026944 | tf_op jit(solution)/shard_map/while/body/eval_jaxpr/hgqk,khd->hgqd/dot_general | solution.py:34
  164.5 3.7 %fusion.125 = f32[1,8,256,128]{3,2,1,0:T(8,128)S(1)} fusion(f32[1024,256,8]{1,0,2:T(8,128)S(1)} %get-tuple-element.722, f32[8,256]{1,0:T(8,128)S(1)} %bitcast.290, pred[256,1024]{0,1:T(8,128)(4,1)S(1)} %fusion.121, f32[1,8,256,128]{3,2,1,0:T(8,128)S(1)} %get-tuple-element.811, f32[8,256]{1,0:T(8,128)S(1)} %get-tuple-element.723, ...), kind=kOutput, calls=%fused_computation.52.clone.1 | convolution fusion | flops 547880960 | bytes 11026944 | tf_op jit(solution)/shard_map/while/body/eval_jaxpr/hgqk,khd->hgqd/dot_general | solution.py:34
  173.8 84.2 %all-gather.8.cloned.1.call-done = bf16[4096,1024]{0,1:T(8,128)(2,1)} async-done(((bf16[256,1024]{0,1:T(8,128)(2,1)}), bf16[4096,1024]{0,1:T(8,128)(2,1)}) %all-gather.8.cloned.1.call-update) | async-done | bytes 8388624 | tf_op jit(solution)/shard_map/all_gather | solution.py:138
  258.0 9.5 %convolution_convert_fusion = bf16[4096,512]{0,1:T(8,128)(2,1)} fusion(bf16[4096,1024]{0,1:T(8,128)(2,1)} %all-gather.8.cloned.1.call-done, bf16[1024,512]{1,0:T(8,128)(2,1)S(1)} %copy-done), kind=kOutput, calls=%fused_computation.113 | convolution fusion | flops 4297064448 | bytes 13631488 | tf_op jit(solution)/shard_map/dot_general | solution.py:137
  267.6 53.6 %reduce-scatter.2.cloned.1.call-done = bf16[4096,64]{0,1:T(8,128)(2,1)} async-done(((bf16[4096,512]{0,1:T(8,128)(2,1)}), bf16[4096,64]{0,1:T(8,128)(2,1)}) %reduce-scatter.2.cloned.1.call-update) | async-done | bytes 524304 | tf_op jit(solution)/shard_map/reduce_scatter | solution.py:143
  322.3 18.5 %all_to_all.19 = bf16[16,256,64]{1,2,0:T(8,128)(2,1)S(1)} all-to-all(bf16[16,256,64]{1,2,0:T(8,128)(2,1)S(1)} %bitcast.294), channel_id=1, replica_groups=mesh['group'=2,'branch'=16,'tensor'=8] {'branch'}, dimensions={0} | all-to-all | bytes 1048576 | tf_op jit(solution)/shard_map/all_to_all | solution.py:146
  (117 shorter events, 60.7 us)
Async XLA Ops:
  6.5 251.5 %copy-start = (bf16[1024,512]{1,0:T(8,128)(2,1)S(1)}, bf16[1024,512]{1,0:T(8,128)(2,1)}, u32[]{:S(2)}) copy-start(bf16[1024,512]{1,0:T(8,128)(2,1)} %param.19) | copy-start | bytes 3145732
  6.5 61.3 %all-gather.4.cloned.1.call-start = ((), (), s32[]{:S(2)}) async-start(), calls=%async_computation.2 | async-start | bytes 2228224 | tf_op jit(solution)/shard_map/all_gather | solution.py:130
  7.3 115.8 %all-gather.6.cloned.1.call-start = ((), (), s32[]{:S(2)}) async-start(), calls=%async_computation.3 | async-start | bytes 2228224 | tf_op jit(solution)/shard_map/all_gather | solution.py:131
  8.0 250.0 %all-gather.8.cloned.1.call-start = ((), (), s32[]{:S(2)}) async-start(), calls=%async_computation.4 | async-start | bytes 8912896 | tf_op jit(solution)/shard_map/all_gather | solution.py:138
  10.8 19.5 %copy-start.2 = (s32[16]{0:T(128)S(1)}, s32[16]{0:T(128)}, u32[]{:S(2)}) copy-start(s32[16]{0:T(128)} %param.18) | copy-start | bytes 196
  14.4 4.6 %copy-start.1 = (f32[768,256,8]{1,0,2:T(8,128)S(1)}, f32[768,256,8]{1,0,2:T(8,128)}, u32[]{:S(2)}) copy-start(f32[768,256,8]{1,0,2:T(8,128)} %get-tuple-element.733) | copy-start | bytes 18874372 | tf_op jit(solution)/shard_map/while
  23.8 4.8 %copy-start.1 = (f32[768,256,8]{1,0,2:T(8,128)S(1)}, f32[768,256,8]{1,0,2:T(8,128)}, u32[]{:S(2)}) copy-start(f32[768,256,8]{1,0,2:T(8,128)} %get-tuple-element.733) | copy-start | bytes 18874372 | tf_op jit(solution)/shard_map/while
  173.8 147.4 %reduce-scatter.2.cloned.1.call-start = ((), (), s32[]{:S(2)}) async-start(), calls=%async_computation.5 | async-start | bytes 4718592 | tf_op jit(solution)/shard_map/reduce_scatter | solution.py:143
Sparse Core Ops, SparseCore 0:
  10.1 57.6 all-gather.3
  70.6 52.3 all-gather.5
  173.9 84.0 all-gather.7
  267.7 53.4 reduce-scatter.1
where the time goes:
time: 349 us; the launch traced here: 348 us
  waiting for transfers between devices  186 us (53%)
  matrix products  77 us (22%)
  other arithmetic  29.6 us (8%)
  local copies, waits for them, and re-layouts  18.5 us (5%)
  blocking collectives  18.5 us (5%)
  between operations  13.2 us (4%)
  loops' own time  5.53 us (2%)
    all_gather x1, waiting for transfers between devices, per_device(): lax.all_gather(attention, 'branch', axis=0, tiled=True)  84.2 us
    reduce_scatter x1, waiting for transfers between devices, per_device(): lax.psum_scatter(partial_columns.astype(jnp.bfloat16), 'tensor', scatter_...  53.6 us
    dot_general x10, matrix products, update_state(): jnp.einsum('hgqk,khd->hgqd', weights.astype(jnp.bfloat16), value_rows, pr...  40.6 us
    all_gather x1, waiting for transfers between devices, per_device(): lax.all_gather(prior_cache, 'branch', axis=1, tiled=True)  37 us
    dot_general x10, matrix products, update_state(): jnp.einsum('qhgd,khd->hgqk', query_heads, key_rows, preferred_element_typ...  26.9 us
    reduce_sum x10, other arithmetic, update_state(): total_new = total_old * factor + jnp.sum(weights, axis=-1)  20.4 us
    all_to_all x1, blocking collectives, per_device(): lax.all_to_all(column_totals, 'branch', split_axis=0, concat_axis=1, tile...  18.5 us
    all_gather x1, waiting for transfers between devices, per_device(): lax.all_gather(fresh_cache, 'branch', axis=1, tiled=True)  9.58 us
  transfers between devices with their start and end apart: 4, of which 4 were waited for; matrix products, arithmetic and copies ran while one was open for 19% of the time, Pallas kernels for 0%

commit v1 on v0

--- a/solution.py
+++ b/solution.py
@@ -124,12 +124,15 @@
         running = sweep(running, query_heads, prior_keys, prior_values, prior_allowed)
         return sweep(running, query_heads, fresh_keys, fresh_values, fresh_allowed)
 
+    def rings_edit(my_tile):
+        fresh = jnp.stack([my_tile for _ in range(lax.axis_size("branch"))])
+        long_array = lax.all_to_all(fresh, "branch", split_axis=0, concat_axis=0)
+        high = jnp.concatenate(long_array, 1)
+        return high
+
     peak_final, total_final, summed_final = add_messages(
         prefix_state,
-        (
-            lax.all_gather(prior_cache, "branch", axis=1, tiled=True),
-            lax.all_gather(fresh_cache, "branch", axis=1, tiled=True),
-        ),
+        (rings_edit(prior_cache), lax.all_gather(fresh_cache, "branch", axis=1, tiled=True)),
         jnp.int32(0),
     )
     heads_out = (summed_final / total_final[..., None]).astype(jnp.bfloat16)

time: 349 us -> 322 us (0.923)
  waiting for transfers between devices: 186 us -> 147 us
  starting transfers between devices: 0.12 us -> 8.56 us
    all_gather x1 -> x0, waiting for transfers between devices: 37 us -> none  [per_device(): lax.all_gather(prior_cache, 'branch', axis=1, tiled=True)]
    all_gather x1, waiting for transfers between devices: 9.58 us -> 0.02 us  [per_device(): lax.all_gather(fresh_cache, 'branch', axis=1, tiled=True)]
    all_to_all x0 -> x1, starting transfers between devices: none -> 8.45 us  [rings_edit(): long_array = lax.all_to_all(fresh, 'branch', split_axis=0, concat_axis=0)]
    all_to_all x0 -> x1, waiting for transfers between devices: none -> 6.11 us  [rings_edit(): long_array = lax.all_to_all(fresh, 'branch', split_axis=0, concat_axis=0)]
  transfers between devices with their start and end apart: 4 -> 4, of which waited for: 4 -> 3; matrix products, arithmetic and copies ran while one was open for 19% -> 20% of each run, Pallas kernels for 0% -> 0%
where the time goes in v1:
time: 322 us; the launch traced here: 321 us
  waiting for transfers between devices  147 us (46%)
  matrix products  77 us (24%)
  other arithmetic  29.9 us (9%)
  local copies, waits for them, and re-layouts  21.5 us (7%)
  blocking collectives  18.5 us (6%)
  between operations  13.2 us (4%)
  starting transfers between devices  8.56 us (3%)
  loops' own time  5.6 us (2%)
    all_gather x1, waiting for transfers between devices, per_device(): lax.all_gather(attention, 'branch', axis=0, tiled=True)  86.7 us
    reduce_scatter x1, waiting for transfers between devices, per_device(): lax.psum_scatter(partial_columns.astype(jnp.bfloat16), 'tensor', scatter_...  53.6 us
    dot_general x10, matrix products, update_state(): jnp.einsum('hgqk,khd->hgqd', weights.astype(jnp.bfloat16), value_rows, pr...  40.6 us
    dot_general x10, matrix products, update_state(): jnp.einsum('qhgd,khd->hgqk', query_heads, key_rows, preferred_element_typ...  26.9 us
    reduce_sum x10, other arithmetic, update_state(): total_new = total_old * factor + jnp.sum(weights, axis=-1)  20.4 us
    all_to_all x1, blocking collectives, per_device(): lax.all_to_all(column_totals, 'branch', split_axis=0, concat_axis=1, tile...  18.5 us
    dot_general x1, matrix products, per_device(): jnp.dot(lax.all_gather(attention, 'branch', axis=0, tiled=True), output_w...  9.55 us
    all_to_all x1, starting transfers between devices, rings_edit(): long_array = lax.all_to_all(fresh, 'branch', split_axis=0, concat_axis=0)  8.45 us
  transfers between devices with their start and end apart: 4, of which 3 were waited for; matrix products, arithmetic and copies ran while one was open for 20% of the time, Pallas kernels for 0%

profile of v1, /device:TPU:1, one launch (start us, length us, event | category | flops | bytes accessed | tf_op | source)
XLA Modules:
  0.0 321.4 jit_solution(4752608446305261824)
XLA Ops:
  6.5 2.8 stack.2
  9.3 8.4 %all-to-all-start = ((bf16[16,2,256,128]{3,2,1,0:T(8,128)(2,1)}), bf16[16,2,256,128]{3,2,1,0:T(8,128)(2,1)}, u32[]{:S(2)}, u32[]{:S(2)}) async-start(bf16[16,2,256,128]{3,2,1,0:T(8,128)(2,1)} %stack.2), calls=%async_computation | async-start | bytes 4194304 | tf_op jit(solution)/shard_map/all_to_all | solution.py:129
  22.6 18.8 %while.51 = (s32[]{:T(128)}, f32[1,8,256]{2,1,0:T(8,128)S(1)}, f32[1,8,256]{2,1,0:T(8,128)S(1)}, f32[1,8,256,128]{3,2,1,0:T(8,128)S(1)}, bf16[2,768,1,128]{3,1,2...) while((s32[]{:T(128)}, f32[1,8,256]{2,1,0:T(8,128)S(1)}, ...), condition=%wide.region_3.4_spmd.clone, body=%wide.region_0.3_spmd.clone.sunk | while | flops 818688000 | bytes 47186060 | solution.py:67
  22.6 3.6 %bitcast_reduce_fusion.5 = (f32[8,256]{1,0:T(8,128)S(1)}, f32[768,256,8]{1,0,2:T(8,128)}) fusion(bf16[256,1,8,128]{3,0,2,1:T(8,128)(2,1)S(1)} %get-tuple-element.785, bf16[2,768,1,128]{3,1,2,0:T(8,128)(2,1)S(1)} %get-tuple-element.784, s32[]{:T(128)} %get-tuple-element.771), kind=kOutput, calls=%fused_computation.88.clone.1 | convolution fusion | flops 405796864 | bytes 7020548 | tf_op jit(solution)/shard_map/while/body/eval_jaxpr/qhgd,khd->hgqk/dot_general | solution.py:21
  26.3 4.5 %fusion.130 = f32[1,8,256,128]{3,2,1,0:T(8,128)S(1)} fusion(f32[768,256,8]{1,0,2:T(8,128)} %get-tuple-element.760, f32[8,256]{1,0:T(8,128)S(1)} %bitcast.289, f32[1,8,256,128]{3,2,1,0:T(8,128)S(1)} %get-tuple-element.774, f32[8,256]{1,0:T(8,128)S(1)} %get-tuple-element.761, pred[]{:T(512)S(6)} %compare.35, ...), kind=kOutput, calls=%fused_computation.97.clone.1 | convolution fusion | flops 408158208 | bytes 8601605 | tf_op jit(solution)/shard_map/while/body/eval_jaxpr/hgqk,khd->hgqd/dot_general | solution.py:34
  32.0 3.6 %bitcast_reduce_fusion.5 = (f32[8,256]{1,0:T(8,128)S(1)}, f32[768,256,8]{1,0,2:T(8,128)}) fusion(bf16[256,1,8,128]{3,0,2,1:T(8,128)(2,1)S(1)} %get-tuple-element.785, bf16[2,768,1,128]{3,1,2,0:T(8,128)(2,1)S(1)} %get-tuple-element.784, s32[]{:T(128)} %get-tuple-element.771), kind=kOutput, calls=%fused_computation.88.clone.1 | convolution fusion | flops 405796864 | bytes 7020548 | tf_op jit(solution)/shard_map/while/body/eval_jaxpr/qhgd,khd->hgqk/dot_general | solution.py:21
  35.6 4.6 %fusion.130 = f32[1,8,256,128]{3,2,1,0:T(8,128)S(1)} fusion(f32[768,256,8]{1,0,2:T(8,128)} %get-tuple-element.760, f32[8,256]{1,0:T(8,128)S(1)} %bitcast.289, f32[1,8,256,128]{3,2,1,0:T(8,128)S(1)} %get-tuple-element.774, f32[8,256]{1,0:T(8,128)S(1)} %get-tuple-element.761, pred[]{:T(512)S(6)} %compare.35, ...), kind=kOutput, calls=%fused_computation.97.clone.1 | convolution fusion | flops 408158208 | bytes 8601605 | tf_op jit(solution)/shard_map/while/body/eval_jaxpr/hgqk,khd->hgqd/dot_general | solution.py:34
  41.4 6.1 %all-to-all-done = bf16[16,2,256,128]{3,2,1,0:T(8,128)(2,1)} async-done(((bf16[16,2,256,128]{3,2,1,0:T(8,128)(2,1)}), bf16[16,2,256,128]{3,2,1,0:T(8,128)(2,1)}, u32[]{:S(2)}, u32[]{:S(2)}) %all-to-all-start) | async-done | bytes 2097184 | tf_op jit(solution)/shard_map/all_to_all | solution.py:129
  47.5 3.1 fusion.93
  50.7 42.8 %while.49 = (s32[]{:T(128)}, f32[1,8,256]{2,1,0:T(8,128)S(1)}, f32[1,8,256]{2,1,0:T(8,128)S(1)}, f32[1,8,256,128]{3,2,1,0:T(8,128)S(1)}, s32[4]{0:T(128)S(1)}, /...) while((s32[]{:T(128)}, f32[1,8,256]{2,1,0:T(8,128)S(1)}, ...), condition=%wide.region_8.9_spmd.clone, body=%wide.region_4.8_spmd.clone.sunk | while | flops 1101600768 | bytes 28465352 | solution.py:67
  54.6 4.2 %fusion.118 = f32[1,8,256,128]{3,2,1,0:T(8,128)S(1)} fusion(f32[1024,256,8]{1,0,2:T(8,128)S(1)} %get-tuple-element.732, f32[8,256]{1,0:T(8,128)S(1)} %bitcast.293, pred[1024]{0:T(1024)(128)(4,1)S(1)} %broadcast_compare_fusion.5, f32[1,8,256,128]{3,2,1,0:T(8,128)S(1)} %get-tuple-element.803, f32[8,256]{1,0:T(8,128)S(1)} %get-tuple-element.733, ...), kind=kOutput, calls=%fused_computation.15.clone.1 | convolution fusion | flops 547880960 | bytes 10766848 | tf_op jit(solution)/shard_map/while/body/eval_jaxpr/hgqk,khd->hgqd/dot_general | solution.py:34
  65.3 4.2 %fusion.118 = f32[1,8,256,128]{3,2,1,0:T(8,128)S(1)} fusion(f32[1024,256,8]{1,0,2:T(8,128)S(1)} %get-tuple-element.732, f32[8,256]{1,0:T(8,128)S(1)} %bitcast.293, pred[1024]{0:T(1024)(128)(4,1)S(1)} %broadcast_compare_fusion.5, f32[1,8,256,128]{3,2,1,0:T(8,128)S(1)} %get-tuple-element.803, f32[8,256]{1,0:T(8,128)S(1)} %get-tuple-element.733, ...), kind=kOutput, calls=%fused_computation.15.clone.1 | convolution fusion | flops 547880960 | bytes 10766848 | tf_op jit(solution)/shard_map/while/body/eval_jaxpr/hgqk,khd->hgqd/dot_general | solution.py:34
  76.0 4.2 %fusion.118 = f32[1,8,256,128]{3,2,1,0:T(8,128)S(1)} fusion(f32[1024,256,8]{1,0,2:T(8,128)S(1)} %get-tuple-element.732, f32[8,256]{1,0:T(8,128)S(1)} %bitcast.293, pred[1024]{0:T(1024)(128)(4,1)S(1)} %broadcast_compare_fusion.5, f32[1,8,256,128]{3,2,1,0:T(8,128)S(1)} %get-tuple-element.803, f32[8,256]{1,0:T(8,128)S(1)} %get-tuple-element.733, ...), kind=kOutput, calls=%fused_computation.15.clone.1 | convolution fusion | flops 547880960 | bytes 10766848 | tf_op jit(solution)/shard_map/while/body/eval_jaxpr/hgqk,khd->hgqd/dot_general | solution.py:34
  86.7 4.2 %fusion.118 = f32[1,8,256,128]{3,2,1,0:T(8,128)S(1)} fusion(f32[1024,256,8]{1,0,2:T(8,128)S(1)} %get-tuple-element.732, f32[8,256]{1,0:T(8,128)S(1)} %bitcast.293, pred[1024]{0:T(1024)(128)(4,1)S(1)} %broadcast_compare_fusion.5, f32[1,8,256,128]{3,2,1,0:T(8,128)S(1)} %get-tuple-element.803, f32[8,256]{1,0:T(8,128)S(1)} %get-tuple-element.733, ...), kind=kOutput, calls=%fused_computation.15.clone.1 | convolution fusion | flops 547880960 | bytes 10766848 | tf_op jit(solution)/shard_map/while/body/eval_jaxpr/hgqk,khd->hgqd/dot_general | solution.py:34
  93.5 3.0 fusion.92
  96.5 44.4 %while.50 = (s32[]{:T(128)}, f32[1,8,256]{2,1,0:T(8,128)S(1)}, f32[1,8,256]{2,1,0:T(8,128)S(1)}, f32[1,8,256,128]{3,2,1,0:T(8,128)S(1)}, s32[4]{0:T(128)S(1)}, /...) while((s32[]{:T(128)}, f32[1,8,256]{2,1,0:T(8,128)S(1)}, ...), condition=%wide.region_13.14_spmd.clone, body=%wide.region_9.13_spmd.clone.sunk | while | flops 1102416896 | bytes 29521128 | solution.py:67
  101.9 3.7 %fusion.125 = f32[1,8,256,128]{3,2,1,0:T(8,128)S(1)} fusion(f32[1024,256,8]{1,0,2:T(8,128)S(1)} %get-tuple-element.749, f32[8,256]{1,0:T(8,128)S(1)} %bitcast.295, pred[256,1024]{0,1:T(8,128)(4,1)S(1)} %fusion.121, f32[1,8,256,128]{3,2,1,0:T(8,128)S(1)} %get-tuple-element.838, f32[8,256]{1,0:T(8,128)S(1)} %get-tuple-element.750, ...), kind=kOutput, calls=%fused_computation.52.clone.1 | convolution fusion | flops 547880960 | bytes 11026944 | tf_op jit(solution)/shard_map/while/body/eval_jaxpr/hgqk,khd->hgqd/dot_general | solution.py:34
  113.0 3.7 %fusion.125 = f32[1,8,256,128]{3,2,1,0:T(8,128)S(1)} fusion(f32[1024,256,8]{1,0,2:T(8,128)S(1)} %get-tuple-element.749, f32[8,256]{1,0:T(8,128)S(1)} %bitcast.295, pred[256,1024]{0,1:T(8,128)(4,1)S(1)} %fusion.121, f32[1,8,256,128]{3,2,1,0:T(8,128)S(1)} %get-tuple-element.838, f32[8,256]{1,0:T(8,128)S(1)} %get-tuple-element.750, ...), kind=kOutput, calls=%fused_computation.52.clone.1 | convolution fusion | flops 547880960 | bytes 11026944 | tf_op jit(solution)/shard_map/while/body/eval_jaxpr/hgqk,khd->hgqd/dot_general | solution.py:34
  124.1 3.7 %fusion.125 = f32[1,8,256,128]{3,2,1,0:T(8,128)S(1)} fusion(f32[1024,256,8]{1,0,2:T(8,128)S(1)} %get-tuple-element.749, f32[8,256]{1,0:T(8,128)S(1)} %bitcast.295, pred[256,1024]{0,1:T(8,128)(4,1)S(1)} %fusion.121, f32[1,8,256,128]{3,2,1,0:T(8,128)S(1)} %get-tuple-element.838, f32[8,256]{1,0:T(8,128)S(1)} %get-tuple-element.750, ...), kind=kOutput, calls=%fused_computation.52.clone.1 | convolution fusion | flops 547880960 | bytes 11026944 | tf_op jit(solution)/shard_map/while/body/eval_jaxpr/hgqk,khd->hgqd/dot_general | solution.py:34
  135.2 3.7 %fusion.125 = f32[1,8,256,128]{3,2,1,0:T(8,128)S(1)} fusion(f32[1024,256,8]{1,0,2:T(8,128)S(1)} %get-tuple-element.749, f32[8,256]{1,0:T(8,128)S(1)} %bitcast.295, pred[256,1024]{0,1:T(8,128)(4,1)S(1)} %fusion.121, f32[1,8,256,128]{3,2,1,0:T(8,128)S(1)} %get-tuple-element.838, f32[8,256]{1,0:T(8,128)S(1)} %get-tuple-element.750, ...), kind=kOutput, calls=%fused_computation.52.clone.1 | convolution fusion | flops 547880960 | bytes 11026944 | tf_op jit(solution)/shard_map/while/body/eval_jaxpr/hgqk,khd->hgqd/dot_general | solution.py:34
  144.4 86.7 %all-gather.5.cloned.1.call-done = bf16[4096,1024]{0,1:T(8,128)(2,1)} async-done(((bf16[256,1024]{0,1:T(8,128)(2,1)}), bf16[4096,1024]{0,1:T(8,128)(2,1)}) %all-gather.5.cloned.1.call-update) | async-done | bytes 8388624 | tf_op jit(solution)/shard_map/all_gather | solution.py:141
  231.1 9.5 %convolution_convert_fusion = bf16[4096,512]{0,1:T(8,128)(2,1)} fusion(bf16[4096,1024]{0,1:T(8,128)(2,1)} %all-gather.5.cloned.1.call-done, bf16[1024,512]{1,0:T(8,128)(2,1)S(1)} %copy-done), kind=kOutput, calls=%fused_computation.113 | convolution fusion | flops 4297064448 | bytes 13631488 | tf_op jit(solution)/shard_map/dot_general | solution.py:140
  240.7 53.6 %reduce-scatter.2.cloned.1.call-done = bf16[4096,64]{0,1:T(8,128)(2,1)} async-done(((bf16[4096,512]{0,1:T(8,128)(2,1)}), bf16[4096,64]{0,1:T(8,128)(2,1)}) %reduce-scatter.2.cloned.1.call-update) | async-done | bytes 524304 | tf_op jit(solution)/shard_map/reduce_scatter | solution.py:146
  295.4 18.5 %all_to_all.24 = bf16[16,256,64]{1,2,0:T(8,128)(2,1)S(1)} all-to-all(bf16[16,256,64]{1,2,0:T(8,128)(2,1)S(1)} %bitcast.299), channel_id=1, replica_groups=mesh['group'=2,'branch'=16,'tensor'=8] {'branch'}, dimensions={0} | all-to-all | bytes 1048576 | tf_op jit(solution)/shard_map/all_to_all | solution.py:149
  (117 shorter events, 62.9 us)
Async XLA Ops:
  6.5 224.6 %copy-start = (bf16[1024,512]{1,0:T(8,128)(2,1)S(1)}, bf16[1024,512]{1,0:T(8,128)(2,1)}, u32[]{:S(2)}) copy-start(bf16[1024,512]{1,0:T(8,128)(2,1)} %param.19) | copy-start | bytes 3145732
  6.5 15.5 %copy-start.2 = (s32[16]{0:T(128)S(1)}, s32[16]{0:T(128)}, u32[]{:S(2)}) copy-start(s32[16]{0:T(128)} %param.18) | copy-start | bytes 196
  9.3 38.2 %all-to-all-start = ((bf16[16,2,256,128]{3,2,1,0:T(8,128)(2,1)}), bf16[16,2,256,128]{3,2,1,0:T(8,128)(2,1)}, u32[]{:S(2)}, u32[]{:S(2)}) async-start(bf16[16,2,256,128]{3,2,1,0:T(8,128)(2,1)} %stack.2), calls=%async_computation | async-start | bytes 4194304 | tf_op jit(solution)/shard_map/all_to_all | solution.py:129
  17.8 75.7 %all-gather.3.cloned.1.call-start = ((), (), s32[]{:S(2)}) async-start(), calls=%async_computation.3 | async-start | bytes 2228224 | tf_op jit(solution)/shard_map/all_gather | solution.py:135
  18.5 212.6 %all-gather.5.cloned.1.call-start = ((), (), s32[]{:S(2)}) async-start(), calls=%async_computation.4 | async-start | bytes 8912896 | tf_op jit(solution)/shard_map/all_gather | solution.py:141
  26.3 4.6 %copy-start.1 = (f32[768,256,8]{1,0,2:T(8,128)S(1)}, f32[768,256,8]{1,0,2:T(8,128)}, u32[]{:S(2)}) copy-start(f32[768,256,8]{1,0,2:T(8,128)} %get-tuple-element.760) | copy-start | bytes 18874372 | tf_op jit(solution)/shard_map/while
  35.6 4.7 %copy-start.1 = (f32[768,256,8]{1,0,2:T(8,128)S(1)}, f32[768,256,8]{1,0,2:T(8,128)}, u32[]{:S(2)}) copy-start(f32[768,256,8]{1,0,2:T(8,128)} %get-tuple-element.760) | copy-start | bytes 18874372 | tf_op jit(solution)/shard_map/while
  144.4 149.9 %reduce-scatter.2.cloned.1.call-start = ((), (), s32[]{:S(2)}) async-start(), calls=%async_computation.5 | async-start | bytes 4718592 | tf_op jit(solution)/shard_map/reduce_scatter | solution.py:146
Sparse Core Ops, SparseCore 0:
  21.4 61.4 all-gather.2
  144.5 86.5 all-gather.4
  240.8 53.4 reduce-scatter.1
